TPU v7x, 32 devices: a whole 2x2x4 slice. The times are simulated.
32 devices in a mesh: row: 8 (over y, x, core), col: 4 (over z).
Axes of the slice: x: 2, y: 2, z: 4, core: 2. Of those that a mesh axis runs over, the one named last changes fastest.
Arguments:
- draws: bfloat16 [128, 16384], P('row', 'col'), may hold values from -6 to 6
- u_factors: bfloat16 [16, 16, 1024, 64], P('row', 'col'), may hold values from -0.1875 to 0.1875
- v_factors: bfloat16 [16, 16, 1024, 64], P('row', 'col'), may hold values from -0.1875 to 0.1875
- ranks: int32 [16, 16], P('row', 'col'), may hold values from 16 to 64
- near: int32 [16, 16], P('row'), may hold values from 0 to 15, as said below
- row_coords: float32 [2, 16384], P(None, 'row'), may hold values from 0 to 4
- col_coords: float32 [2, 16384], replicated, may hold values from 0 to 4
Outputs:
- applied: float32 [128, 16384], P('col', 'row')
Inputs may be any that keep to these rules, and one draw needn't show every extreme that they name: `ranks`: the rank of a tile; factor columns from its rank on are padding. `near`: each block row lists 16 different block columns.
All inputs are finite; a program needn't handle non-finite values.
Results may differ from a plain program's by a relative error of at most 0.0029.
Values may be sent and summed in bfloat16 or wider, within the bound.
A program may use at most 64 MiB of HBM per device.

v0:
```python
import jax
import jax.numpy as jnp
from jax import lax
from jax.sharding import PartitionSpec as P


def matern_tile(col_part, row_part):
    delta_x = col_part[0][:, None] - row_part[0][None, :]
    delta_y = col_part[1][:, None] - row_part[1][None, :]
    kernel = jnp.exp(-jnp.sqrt(delta_x * delta_x + delta_y * delta_y)) * 0.03125
    return kernel.astype(jnp.bfloat16)


def per_device(draws, u_factors, v_factors, ranks, near, row_coords, col_coords):
    rows_local, cols_local, tile, rank = u_factors.shape
    first_col = lax.axis_index("col") * cols_local
    whole = lax.all_gather(draws, "row", axis=0, tiled=True)
    width = whole.shape[0]
    column_ids = first_col + jnp.arange(cols_local, dtype=jnp.int32)
    flagged = jnp.any(near[:, :, None] == column_ids[None, None, :], axis=1)
    keep = (jnp.arange(rank, dtype=jnp.int32)[None, None, :] < ranks[:, :, None]) & jnp.logical_not(
        flagged
    )[:, :, None]
    blocks = whole.reshape(width, cols_local, tile)
    reduced = jnp.einsum("nbt,abtk->nabk", blocks, v_factors, preferred_element_type=jnp.float32)
    reduced = jnp.where(keep[None], reduced, 0.0).astype(jnp.bfloat16)
    partial_value = jnp.einsum(
        "nabk,abtk->nat", reduced, u_factors, preferred_element_type=jnp.float32
    )
    partial_value = partial_value.reshape(width, rows_local * tile)
    local_cols = lax.dynamic_slice_in_dim(col_coords, first_col * tile, cols_local * tile, 1)

    def add_tile(step, total):
        row_pos = step // cols_local
        col_pos = step % cols_local

        def dense(acc):
            tile_matrix = matern_tile(
                lax.dynamic_slice_in_dim(local_cols, col_pos * tile, tile, 1),
                lax.dynamic_slice_in_dim(row_coords, row_pos * tile, tile, 1),
            )
            piece = lax.dynamic_slice_in_dim(whole, col_pos * tile, tile, 1)
            product = jnp.dot(piece, tile_matrix, preferred_element_type=jnp.float32)
            current = lax.dynamic_slice_in_dim(acc, row_pos * tile, tile, 1)
            return lax.dynamic_update_slice_in_dim(acc, current + product, row_pos * tile, 1)

        return lax.cond(flagged[row_pos, col_pos], dense, lambda acc: acc, total)

    partial_value = lax.fori_loop(0, rows_local * cols_local, add_tile, partial_value)
    result = lax.psum_scatter(partial_value, "col", scatter_dimension=0, tiled=True)
    return result


def solution(mesh):
    return jax.shard_map(
        per_device,
        mesh=mesh,
        in_specs=(
            P("row", "col"),
            P("row", "col", None, None),
            P("row", "col", None, None),
            P("row", "col"),
            P("row", None),
            P(None, "row"),
            P(),
        ),
        out_specs=P("col", "row"),
        check_vma=False,
    )
```

profile of v0, /device:TPU:0, one launch (start us, length us, event | category | flops | bytes accessed | tf_op | source)
XLA Modules:
  0.0 113.5 jit_solution(2657741215018567093)
XLA Ops:
  7.3 0.9 compare_reduce_fusion
  9.0 0.8 constant_dynamic-slice_fusion.2
  9.7 25.8 %all-gather.2.cloned.1.call-done = bf16[128,4096]{1,0:T(8,128)(2,1)} async-done(((bf16[16,4096]{1,0:T(8,128)(2,1)}), bf16[128,4096]{1,0:T(8,128)(2,1)}) %all-gather.2.cloned.1.call-update) | async-done | bytes 1048592 | tf_op jit(solution)/shard_map/all_gather | solution.py:17
  35.5 1.6 %copy.17 = bf16[128,4096]{0,1:T(8,128)(2,1)S(1)} copy(bf16[128,4096]{1,0:T(8,128)(2,1)} %all-gather.2.cloned.1.call-done) | data formatting | bytes 2097152 | tf_op jit(solution)/shard_map/all_gather | solution.py:17
  37.1 2.0 %convolution_bitcast_fusion = f32[128,2,1024]{2,0,1:T(8,128)S(1)} fusion(bf16[2,4,1024,64]{2,3,1,0:T(8,128)(2,1)S(1)} %copy-done, bf16[2,4,1024,64]{2,3,1,0:T(8,128)(2,1)} %param.13, bf16[128,4,1024,1]{0,2,1,3:T(8,128)(2,1)S(1)} %bitcast.27, pred[2,4,64]{2,1,0:T(4,128)(4,1)S(1)} %fusion.10), kind=kOutput, calls=%fused_computation.9 | convolution fusion | flops 268566528 | bytes 4194816 | tf_op jit(solution)/shard_map/nabk,abtk->nat/dot_general | solution.py:27
  40.2 38.2 %while.18 = (s32[]{:T(128)}, f32[128,2048]{1,0:T(8,128)S(1)}, pred[2,4]{1,0:T(4,128)(4,1)S(1)}, bf16[128,4096]{1,0:T(8,128)(2,1)}, f32[2,4096]{1,0:T(2,128)S(1)}...) while((s32[]{:T(128)}, f32[128,2048]{1,0:T(8,128)S(1)}, ...), condition=%wide.region_4.5_spmd, body=%wide.region_1.4_spmd.sunk | while | flops 276955168 | bytes 1360371 | solution.py:49
  41.4 3.5 %conditional.2 = (f32[128,2048]{1,0:T(8,128)S(1)}) conditional(s32[]{:T(128)} %bitcast.26, f32[128,2048]{1,0:T(8,128)S(1)} %get-tuple-element.284, (s32[]{:T(128)}, f32[128,2048]{1,0:T(8,128)S(1)}, s32[]{:T(128)}, bf16[128,4096]{1,0:T(8,128)(2,1)}, f32[2,4096]{1,0:T(2,128)S(1)}, /*index=5*/f32[2,2048]{1,0:T(2,128)S(1)}) %tuple.58), branch_computations={%region_2.2_spmd, %region_3.3_spmd} | conditional | flops 276955136 | bytes 1360004 | solution.py:47
  41.5 3.4 %fusion.2 = f32[128,2048]{1,0:T(8,128)S(1)} fusion(f32[128,2048]{1,0:T(8,128)S(1)} %get-tuple-element.177, s32[]{:T(128)S(6)} %select_n.60, f32[1024]{0:T(1024)S(1)} %bitcast.30, f32[1024]{0:T(1024)S(1)} %bitcast.31, f32[1024]{0:T(1024)S(1)} %bitcast.29, f32[1024]{0:T(1024)S(1)} %bitcast.32, bf16[128,4096]{1,0:T(8,128)(2,1)} %get-tuple-element.179, ...), kind=kOutput, calls=%fused_computation.3 | convolution fusion | flops 276955136 | bytes 1327112 | tf_op jit(solution)/shard_map/while/body/eval_jaxpr/cond/branch_1_fun/dot_general | solution.py:43
  46.2 3.5 %conditional.2 = (f32[128,2048]{1,0:T(8,128)S(1)}) conditional(s32[]{:T(128)} %bitcast.26, f32[128,2048]{1,0:T(8,128)S(1)} %get-tuple-element.284, (s32[]{:T(128)}, f32[128,2048]{1,0:T(8,128)S(1)}, s32[]{:T(128)}, bf16[128,4096]{1,0:T(8,128)(2,1)}, f32[2,4096]{1,0:T(2,128)S(1)}, /*index=5*/f32[2,2048]{1,0:T(2,128)S(1)}) %tuple.58), branch_computations={%region_2.2_spmd, %region_3.3_spmd} | conditional | flops 276955136 | bytes 1360004 | solution.py:47
  46.3 3.4 %fusion.2 = f32[128,2048]{1,0:T(8,128)S(1)} fusion(f32[128,2048]{1,0:T(8,128)S(1)} %get-tuple-element.177, s32[]{:T(128)S(6)} %select_n.60, f32[1024]{0:T(1024)S(1)} %bitcast.30, f32[1024]{0:T(1024)S(1)} %bitcast.31, f32[1024]{0:T(1024)S(1)} %bitcast.29, f32[1024]{0:T(1024)S(1)} %bitcast.32, bf16[128,4096]{1,0:T(8,128)(2,1)} %get-tuple-element.179, ...), kind=kOutput, calls=%fused_computation.3 | convolution fusion | flops 276955136 | bytes 1327112 | tf_op jit(solution)/shard_map/while/body/eval_jaxpr/cond/branch_1_fun/dot_general | solution.py:43
  51.0 3.5 %conditional.2 = (f32[128,2048]{1,0:T(8,128)S(1)}) conditional(s32[]{:T(128)} %bitcast.26, f32[128,2048]{1,0:T(8,128)S(1)} %get-tuple-element.284, (s32[]{:T(128)}, f32[128,2048]{1,0:T(8,128)S(1)}, s32[]{:T(128)}, bf16[128,4096]{1,0:T(8,128)(2,1)}, f32[2,4096]{1,0:T(2,128)S(1)}, /*index=5*/f32[2,2048]{1,0:T(2,128)S(1)}) %tuple.58), branch_computations={%region_2.2_spmd, %region_3.3_spmd} | conditional | flops 276955136 | bytes 1360004 | solution.py:47
  51.1 3.4 %fusion.2 = f32[128,2048]{1,0:T(8,128)S(1)} fusion(f32[128,2048]{1,0:T(8,128)S(1)} %get-tuple-element.177, s32[]{:T(128)S(6)} %select_n.60, f32[1024]{0:T(1024)S(1)} %bitcast.30, f32[1024]{0:T(1024)S(1)} %bitcast.31, f32[1024]{0:T(1024)S(1)} %bitcast.29, f32[1024]{0:T(1024)S(1)} %bitcast.32, bf16[128,4096]{1,0:T(8,128)(2,1)} %get-tuple-element.179, ...), kind=kOutput, calls=%fused_computation.3 | convolution fusion | flops 276955136 | bytes 1327112 | tf_op jit(solution)/shard_map/while/body/eval_jaxpr/cond/branch_1_fun/dot_general | solution.py:43
  55.7 3.5 %conditional.2 = (f32[128,2048]{1,0:T(8,128)S(1)}) conditional(s32[]{:T(128)} %bitcast.26, f32[128,2048]{1,0:T(8,128)S(1)} %get-tuple-element.284, (s32[]{:T(128)}, f32[128,2048]{1,0:T(8,128)S(1)}, s32[]{:T(128)}, bf16[128,4096]{1,0:T(8,128)(2,1)}, f32[2,4096]{1,0:T(2,128)S(1)}, /*index=5*/f32[2,2048]{1,0:T(2,128)S(1)}) %tuple.58), branch_computations={%region_2.2_spmd, %region_3.3_spmd} | conditional | flops 276955136 | bytes 1360004 | solution.py:47
  55.9 3.4 %fusion.2 = f32[128,2048]{1,0:T(8,128)S(1)} fusion(f32[128,2048]{1,0:T(8,128)S(1)} %get-tuple-element.177, s32[]{:T(128)S(6)} %select_n.60, f32[1024]{0:T(1024)S(1)} %bitcast.30, f32[1024]{0:T(1024)S(1)} %bitcast.31, f32[1024]{0:T(1024)S(1)} %bitcast.29, f32[1024]{0:T(1024)S(1)} %bitcast.32, bf16[128,4096]{1,0:T(8,128)(2,1)} %get-tuple-element.179, ...), kind=kOutput, calls=%fused_computation.3 | convolution fusion | flops 276955136 | bytes 1327112 | tf_op jit(solution)/shard_map/while/body/eval_jaxpr/cond/branch_1_fun/dot_general | solution.py:43
  60.5 3.5 %conditional.2 = (f32[128,2048]{1,0:T(8,128)S(1)}) conditional(s32[]{:T(128)} %bitcast.26, f32[128,2048]{1,0:T(8,128)S(1)} %get-tuple-element.284, (s32[]{:T(128)}, f32[128,2048]{1,0:T(8,128)S(1)}, s32[]{:T(128)}, bf16[128,4096]{1,0:T(8,128)(2,1)}, f32[2,4096]{1,0:T(2,128)S(1)}, /*index=5*/f32[2,2048]{1,0:T(2,128)S(1)}) %tuple.58), branch_computations={%region_2.2_spmd, %region_3.3_spmd} | conditional | flops 276955136 | bytes 1360004 | solution.py:47
  60.6 3.4 %fusion.2 = f32[128,2048]{1,0:T(8,128)S(1)} fusion(f32[128,2048]{1,0:T(8,128)S(1)} %get-tuple-element.177, s32[]{:T(128)S(6)} %select_n.60, f32[1024]{0:T(1024)S(1)} %bitcast.30, f32[1024]{0:T(1024)S(1)} %bitcast.31, f32[1024]{0:T(1024)S(1)} %bitcast.29, f32[1024]{0:T(1024)S(1)} %bitcast.32, bf16[128,4096]{1,0:T(8,128)(2,1)} %get-tuple-element.179, ...), kind=kOutput, calls=%fused_computation.3 | convolution fusion | flops 276955136 | bytes 1327112 | tf_op jit(solution)/shard_map/while/body/eval_jaxpr/cond/branch_1_fun/dot_general | solution.py:43
  65.3 3.5 %conditional.2 = (f32[128,2048]{1,0:T(8,128)S(1)}) conditional(s32[]{:T(128)} %bitcast.26, f32[128,2048]{1,0:T(8,128)S(1)} %get-tuple-element.284, (s32[]{:T(128)}, f32[128,2048]{1,0:T(8,128)S(1)}, s32[]{:T(128)}, bf16[128,4096]{1,0:T(8,128)(2,1)}, f32[2,4096]{1,0:T(2,128)S(1)}, /*index=5*/f32[2,2048]{1,0:T(2,128)S(1)}) %tuple.58), branch_computations={%region_2.2_spmd, %region_3.3_spmd} | conditional | flops 276955136 | bytes 1360004 | solution.py:47
  65.4 3.4 %fusion.2 = f32[128,2048]{1,0:T(8,128)S(1)} fusion(f32[128,2048]{1,0:T(8,128)S(1)} %get-tuple-element.177, s32[]{:T(128)S(6)} %select_n.60, f32[1024]{0:T(1024)S(1)} %bitcast.30, f32[1024]{0:T(1024)S(1)} %bitcast.31, f32[1024]{0:T(1024)S(1)} %bitcast.29, f32[1024]{0:T(1024)S(1)} %bitcast.32, bf16[128,4096]{1,0:T(8,128)(2,1)} %get-tuple-element.179, ...), kind=kOutput, calls=%fused_computation.3 | convolution fusion | flops 276955136 | bytes 1327112 | tf_op jit(solution)/shard_map/while/body/eval_jaxpr/cond/branch_1_fun/dot_general | solution.py:43
  70.1 3.5 %conditional.2 = (f32[128,2048]{1,0:T(8,128)S(1)}) conditional(s32[]{:T(128)} %bitcast.26, f32[128,2048]{1,0:T(8,128)S(1)} %get-tuple-element.284, (s32[]{:T(128)}, f32[128,2048]{1,0:T(8,128)S(1)}, s32[]{:T(128)}, bf16[128,4096]{1,0:T(8,128)(2,1)}, f32[2,4096]{1,0:T(2,128)S(1)}, /*index=5*/f32[2,2048]{1,0:T(2,128)S(1)}) %tuple.58), branch_computations={%region_2.2_spmd, %region_3.3_spmd} | conditional | flops 276955136 | bytes 1360004 | solution.py:47
  70.2 3.4 %fusion.2 = f32[128,2048]{1,0:T(8,128)S(1)} fusion(f32[128,2048]{1,0:T(8,128)S(1)} %get-tuple-element.177, s32[]{:T(128)S(6)} %select_n.60, f32[1024]{0:T(1024)S(1)} %bitcast.30, f32[1024]{0:T(1024)S(1)} %bitcast.31, f32[1024]{0:T(1024)S(1)} %bitcast.29, f32[1024]{0:T(1024)S(1)} %bitcast.32, bf16[128,4096]{1,0:T(8,128)(2,1)} %get-tuple-element.179, ...), kind=kOutput, calls=%fused_computation.3 | convolution fusion | flops 276955136 | bytes 1327112 | tf_op jit(solution)/shard_map/while/body/eval_jaxpr/cond/branch_1_fun/dot_general | solution.py:43
  74.8 3.5 %conditional.2 = (f32[128,2048]{1,0:T(8,128)S(1)}) conditional(s32[]{:T(128)} %bitcast.26, f32[128,2048]{1,0:T(8,128)S(1)} %get-tuple-element.284, (s32[]{:T(128)}, f32[128,2048]{1,0:T(8,128)S(1)}, s32[]{:T(128)}, bf16[128,4096]{1,0:T(8,128)(2,1)}, f32[2,4096]{1,0:T(2,128)S(1)}, /*index=5*/f32[2,2048]{1,0:T(2,128)S(1)}) %tuple.58), branch_computations={%region_2.2_spmd, %region_3.3_spmd} | conditional | flops 276955136 | bytes 1360004 | solution.py:47
  75.0 3.4 %fusion.2 = f32[128,2048]{1,0:T(8,128)S(1)} fusion(f32[128,2048]{1,0:T(8,128)S(1)} %get-tuple-element.177, s32[]{:T(128)S(6)} %select_n.60, f32[1024]{0:T(1024)S(1)} %bitcast.30, f32[1024]{0:T(1024)S(1)} %bitcast.31, f32[1024]{0:T(1024)S(1)} %bitcast.29, f32[1024]{0:T(1024)S(1)} %bitcast.32, bf16[128,4096]{1,0:T(8,128)(2,1)} %get-tuple-element.179, ...), kind=kOutput, calls=%fused_computation.3 | convolution fusion | flops 276955136 | bytes 1327112 | tf_op jit(solution)/shard_map/while/body/eval_jaxpr/cond/branch_1_fun/dot_general | solution.py:43
  78.3 1.0 copy-done.1
  79.3 27.3 %reduce-scatter.2.cloned.1.call-done = f32[32,2048]{1,0:T(8,128)} async-done(((f32[128,2048]{1,0:T(8,128)}), f32[32,2048]{1,0:T(8,128)}) %reduce-scatter.2.cloned.1.call-update) | async-done | bytes 262160 | tf_op jit(solution)/shard_map/reduce_scatter | solution.py:50
  (30 shorter events, 8.2 us)
Async XLA Ops:
  6.5 30.6 %copy-start = (bf16[2,4,1024,64]{2,3,1,0:T(8,128)(2,1)S(1)}, bf16[2,4,1024,64]{2,3,1,0:T(8,128)(2,1)}, u32[]{:S(2)}) copy-start(bf16[2,4,1024,64]{2,3,1,0:T(8,128)(2,1)} %param.12) | copy-start | bytes 3145732
  6.5 28.9 %all-gather.2.cloned.1.call-start = ((), (), s32[]{:S(2)}) async-start(), calls=%async_computation.1 | async-start | bytes 1179648 | tf_op jit(solution)/shard_map/all_gather | solution.py:17
  7.3 99.4 %reduce-scatter.2.cloned.1.call-start = ((), (), s32[]{:S(2)}) async-start(), calls=%async_computation.2 | async-start | bytes 1310720 | tf_op jit(solution)/shard_map/reduce_scatter | solution.py:50
  39.4 0.7 copy-start.2
  78.3 1.0 copy-start.1
Sparse Core Ops, SparseCore 0:
  9.2 26.1 all-gather.1
  79.4 27.1 reduce-scatter.1
where the time goes:
time: 114 us; the launch traced here: 113 us
  waiting for transfers between devices  53.8 us (47%)
  matrix products  28.9 us (25%)
  between operations  13.5 us (12%)
  local copies, waits for them, and re-layouts  10 us (9%)
  loops' own time  5.64 us (5%)
  other arithmetic  1.63 us (1%)
    reduce_scatter x1, waiting for transfers between devices, per_device(): lax.psum_scatter(partial_value, 'col', scatter_dimension=0, tiled=True)  27.3 us
    dot_general x8, matrix products, dense(): product = jnp.dot(piece, tile_matrix, preferred_element_type=jnp.float32)  26.9 us
    all_gather x1, waiting for transfers between devices, per_device(): whole = lax.all_gather(draws, 'row', axis=0, tiled=True)  25.8 us
    another operation x1, loops' own time, per_device(): lax.fori_loop(0, rows_local * cols_local, add_tile, partial_value)  5.41 us
    dynamic_slice x8, local copies, waits for them, and re-layouts, add_tile(): return lax.cond(flagged[row_pos, col_pos], dense, lambda acc: acc, total)  4.91 us
  transfers between devices with their start and end apart: 2, of which 2 were waited for; matrix products, arithmetic and copies ran while one was open for 2% of the time, Pallas kernels for 0%

commit v1 on v0

--- a/solution.py
+++ b/solution.py
@@ -1,7 +1,17 @@
+import functools
+
 import jax
 import jax.numpy as jnp
 from jax import lax
+from jax.experimental import pallas as pl
+from jax.experimental.pallas import tpu as pltpu
 from jax.sharding import PartitionSpec as P
+
+MESH = pl.DeviceIdType.MESH
+LOG2E = 1.4426950408889634
+TINY = 1e-12
+WIDE = 256
+TERMS = 32
 
 
 def matern_tile(col_part, row_part):
@@ -51,9 +61,260 @@
     return result
 
 
+def split3(value):
+    high = value.astype(jnp.bfloat16).astype(jnp.float32)
+    rest = value - high
+    middle = rest.astype(jnp.bfloat16).astype(jnp.float32)
+    return high, middle, rest - middle
+
+
+def write_terms(target, coords, is_row):
+    target[...] = jnp.zeros_like(target)
+    x = (coords[0:1, :] - 2.0) * LOG2E
+    y = (coords[1:2, :] - 2.0) * LOG2E
+    norm = split3(x * x + y * y)
+    at = 0
+    order = (0, 1, 0, 2, 0, 1) if is_row else (0, 0, 1, 0, 2, 1)
+    for value in (x, y):
+        parts = split3(value)
+        for piece in order:
+            target[at : at + 1, :] = parts[piece] * -2.0 if is_row else parts[piece]
+            at += 1
+    ones = jnp.ones_like(x)
+    for piece in range(3):
+        target[at : at + 1, :] = ones if is_row else norm[piece]
+        target[at + 3 : at + 4, :] = norm[piece] if is_row else ones
+        at += 1
+
+
+def kernel(
+    cols, draws, u_hbm, v_hbm, ranks, near, row_coords, col_coords, out,
+    u, v, whole, dense, col_terms, col_left, row_terms, red, total, mail, inbox, own,
+    factor_sem, gs_sem, gr_sem, ss_sem, sr_sem,
+):
+    groups, part_rows, width = whole.shape[0], whole.shape[1], whole.shape[2]
+    rows_local, cols_local, tile, rank = u.shape
+    nrhs = groups * part_rows
+    share = nrhs // cols
+    chunks = rows_local * tile // WIDE
+    per_row = tile // WIDE
+    row = lax.axis_index("row")
+    col = lax.axis_index("col")
+    first = col * cols_local
+
+    sibling = row + 1 - 2 * (row % 2)
+    beside = row + 2 - 4 * ((row // 2) % 2)
+    above = row + 4 - 8 * ((row // 4) % 2)
+    across = beside + 4 - 8 * ((row // 4) % 2)
+
+    def other(index):
+        return index + 1 - 2 * (index % 2)
+
+    barrier = pltpu.get_barrier_semaphore()
+    for peer in (sibling, beside, above, across):
+        pl.semaphore_signal(barrier, inc=1, device_id=(peer, col), device_id_type=MESH)
+    for step in range(1, cols):
+        pl.semaphore_signal(barrier, inc=1, device_id=(row, (col + step) % cols), device_id_type=MESH)
+
+    u_copy = pltpu.make_async_copy(u_hbm, u, factor_sem.at[0])
+    v_copy = pltpu.make_async_copy(v_hbm, v, factor_sem.at[1])
+    u_copy.start()
+    v_copy.start()
+
+    write_terms(col_terms, col_coords[:, pl.ds(pl.multiple_of(first * tile, tile), width)], False)
+    write_terms(row_terms, row_coords[...], True)
+    for block in range(width // WIDE):
+        span = slice(block * WIDE, (block + 1) * WIDE)
+        col_left[span, :] = jnp.transpose(col_terms[:, span]).astype(jnp.bfloat16)
+    whole[row] = draws[...]
+    pl.semaphore_wait(barrier, 3 + cols)
+
+    def gather(source, slot, peer, index):
+        return pltpu.make_async_remote_copy(
+            src_ref=source, dst_ref=whole.at[slot], send_sem=gs_sem.at[index],
+            recv_sem=gr_sem.at[index], device_id=(peer, col), device_id_type=MESH,
+        )
+
+    firsts = [gather(draws, row, peer, index) for index, peer in enumerate((beside, above, across, sibling))]
+    for copy in firsts:
+        copy.start()
+
+    def gen(chunk, j, quarter):
+        right = row_terms[:, chunk * WIDE : (chunk + 1) * WIDE].astype(jnp.bfloat16)
+        for half in range(2):
+            at = pl.multiple_of(j * tile + quarter * WIDE + half * 128, 128)
+            squared = jnp.dot(col_left[pl.ds(at, 128), :], right, preferred_element_type=jnp.float32)
+            squared = jnp.maximum(squared, TINY)
+            value = jnp.exp2(-(squared * lax.rsqrt(squared)))
+            dense[chunk, pl.ds(at, 128), :] = value.astype(jnp.bfloat16)
+
+    def flag(i, j):
+        hit = jnp.where(near[i : i + 1, :] == first + j, 1.0, 0.0)
+        return jnp.max(hit, axis=1, keepdims=True)
+
+    def mul(chunk, j, quarter):
+        at = pl.multiple_of(j * tile + quarter * WIDE, WIDE)
+        left = whole[:, :, pl.ds(at, WIDE)].reshape(nrhs, WIDE)
+        return jnp.dot(left, dense[chunk, pl.ds(at, WIDE), :], preferred_element_type=jnp.float32)
+
+    def step(makes, takes):
+        for take in takes:
+            total[take % 2] = jnp.zeros_like(total[take % 2])
+
+        def body(j, carry):
+            sums = [None for _ in takes]
+            for quarter in range(tile // WIDE):
+                for make in makes:
+                    gen(make, j, quarter)
+                for n, take in enumerate(takes):
+                    product = mul(take, j, quarter)
+                    sums[n] = product if sums[n] is None else sums[n] + product
+            for n, take in enumerate(takes):
+                total[take % 2] += sums[n] * flag(take // per_row, j)
+            return carry
+
+        lax.fori_loop(0, cols_local, body, 0)
+        for take in takes:
+            send(take)
+
+    def delivery(chunk, step):
+        peer = (col + step) % cols
+        return pltpu.make_async_remote_copy(
+            src_ref=mail.at[chunk, peer], dst_ref=inbox.at[chunk, step - 1],
+            send_sem=ss_sem.at[chunk, step - 1], recv_sem=sr_sem.at[chunk, step - 1],
+            device_id=(row, peer), device_id_type=MESH,
+        )
+
+    def send(chunk):
+        i = chunk // per_row
+        base = (chunk % per_row) * WIDE
+        value = total[chunk % 2] * 0.03125
+        for j in range(cols_local):
+            value = value + lax.dot_general(
+                red[i, j], u[i, j, base : base + WIDE, :], (((1,), (1,)), ((), ())),
+                preferred_element_type=jnp.float32,
+            )
+        value = value.reshape(cols, share, WIDE)
+        mail[chunk] = value.astype(jnp.bfloat16)
+        own[chunk] = value
+        for step in range(1, cols):
+            delivery(chunk, step).start()
+
+    def receive(chunk):
+        value = own[chunk, col]
+        for step in range(1, cols):
+            delivery(chunk, step).wait_recv()
+            value = value + inbox[chunk, step - 1].astype(jnp.float32)
+        out[:, chunk * WIDE : (chunk + 1) * WIDE] = value
+
+    for phase in PLAN:
+        kind = phase[0]
+        if kind == "step":
+            step(phase[1], phase[2])
+        elif kind == "forward":
+            for index in phase[1]:
+                firsts[index].wait_recv()
+                slot = (beside, above, across)[index]
+                gather(whole.at[slot], slot, sibling, 4 + index).start()
+        elif kind == "ready":
+            for index in range(3):
+                slot = other((beside, above, across)[index])
+                gather(whole.at[slot], slot, sibling, 4 + index).wait_recv()
+            firsts[3].wait_recv()
+        elif kind == "reduce":
+            u_copy.wait()
+            v_copy.wait()
+            for j in range(cols_local):
+                left = whole[:, :, j * tile : (j + 1) * tile].reshape(nrhs, tile)
+                for i in range(rows_local):
+                    value = jnp.dot(left, v[i, j], preferred_element_type=jnp.float32)
+                    index = lax.broadcasted_iota(jnp.int32, value.shape, 1)
+                    keep = jnp.where(index < ranks[i : i + 1, j : j + 1], 1.0, 0.0) * (1.0 - flag(i, j))
+                    red[i, j] = jnp.where(keep > 0.5, value, 0.0).astype(jnp.bfloat16)
+        elif kind == "receive":
+            for chunk in phase[1]:
+                receive(chunk)
+
+    for copy in firsts:
+        copy.wait_send()
+    for index in range(3):
+        slot = (beside, above, across)[index]
+        gather(whole.at[slot], slot, sibling, 4 + index).wait_send()
+    for chunk in range(chunks):
+        for step_at in range(1, cols):
+            delivery(chunk, step_at).wait_send()
+
+
+PLAN = (
+    ("step", (0,), ()),
+    ("step", (1,), ()),
+    ("forward", (0, 1)),
+    ("step", (2,), ()),
+    ("forward", (2,)),
+    ("step", (3,), ()),
+    ("ready",),
+    ("reduce",),
+    ("step", (4,), (0, 1)),
+    ("step", (5,), (2, 3)),
+    ("step", (6,), (4, 5)),
+    ("receive", (0, 1)),
+    ("step", (7,), (6,)),
+    ("receive", (2, 3)),
+    ("step", (), (7,)),
+    ("receive", (4, 5, 6, 7)),
+)
+
+
+def fused(rows, cols, draws, u_factors, v_factors, ranks, near, row_coords, col_coords):
+    part_rows, width = draws.shape
+    rows_local, cols_local, tile, rank = u_factors.shape
+    nrhs = part_rows * rows
+    share = nrhs // cols
+    chunks = rows_local * tile // WIDE
+    vmem = pl.BlockSpec(memory_space=pltpu.VMEM)
+    hbm = pl.BlockSpec(memory_space=pl.ANY)
+    return pl.pallas_call(
+        functools.partial(kernel, cols),
+        out_shape=jax.ShapeDtypeStruct((share, rows_local * tile), jnp.float32),
+        in_specs=[vmem, hbm, hbm, vmem, vmem, vmem, vmem],
+        out_specs=vmem,
+        scratch_shapes=[
+            pltpu.VMEM(u_factors.shape, jnp.bfloat16),
+            pltpu.VMEM(v_factors.shape, jnp.bfloat16),
+            pltpu.VMEM((rows, part_rows, width), jnp.bfloat16),
+            pltpu.VMEM((chunks, width, WIDE), jnp.bfloat16),
+            pltpu.VMEM((TERMS, width), jnp.float32),
+            pltpu.VMEM((width, TERMS), jnp.bfloat16),
+            pltpu.VMEM((TERMS, rows_local * tile), jnp.float32),
+            pltpu.VMEM((rows_local, cols_local, nrhs, rank), jnp.bfloat16),
+            pltpu.VMEM((2, nrhs, WIDE), jnp.float32),
+            pltpu.VMEM((chunks, cols, share, WIDE), jnp.bfloat16),
+            pltpu.VMEM((chunks, cols - 1, share, WIDE), jnp.bfloat16),
+            pltpu.VMEM((chunks, cols, share, WIDE), jnp.float32),
+            pltpu.SemaphoreType.DMA((2,)),
+            pltpu.SemaphoreType.DMA((7,)),
+            pltpu.SemaphoreType.DMA((7,)),
+            pltpu.SemaphoreType.DMA((chunks, cols - 1)),
+            pltpu.SemaphoreType.DMA((chunks, cols - 1)),
+        ],
+        compiler_params=pltpu.CompilerParams(
+            collective_id=0, has_side_effects=True, vmem_limit_bytes=48 * 1024 * 1024
+        ),
+        cost_estimate=pl.CostEstimate(flops=10**10, bytes_accessed=10**7, transcendentals=2 * 10**7),
+    )(draws, u_factors, v_factors, ranks, near, row_coords, col_coords)
+
+
 def solution(mesh):
+    rows, cols = mesh.shape["row"], mesh.shape["col"]
+
+    def local(*args):
+        share = args[0].shape[0] * rows // cols
+        if rows == 8 and cols == 4 and args[0].shape[0] % 16 == 0 and share % 16 == 0 and args[1].shape[:3] == (2, 4, 1024):
+            return fused(rows, cols, *args)
+        return per_device(*args)
+
     return jax.shard_map(
-        per_device,
+        local,
         mesh=mesh,
         in_specs=(
             P("row", "col"),

time: 114 us -> 45.5 us (0.40)
  waiting for transfers between devices: 53.8 us -> 0 us
  Pallas kernels: 0 us -> 39 us
  matrix products: 28.9 us -> 0 us
  between operations: 13.5 us -> 0.09 us
  loops' own time: 5.64 us -> 0 us
  local copies, waits for them, and re-layouts: 10 us -> 6.27 us
  other arithmetic: 1.63 us -> 0 us
    pallas_call x0 -> x1, Pallas kernels: none -> 39 us  [fused(): pl.pallas_call(functools.partial(kernel, cols), out_shape=jax.ShapeDtypeS...]
    dot_general x9 -> x0, matrix products: 28.9 us -> none  [the longest x8 26.9 us: dense(): product = jnp.dot(piece, tile_matrix, preferred_element_type=jnp.float32)]
    reduce_scatter x1 -> x0, waiting for transfers between devices: 27.3 us -> none  [per_device(): lax.psum_scatter(partial_value, 'col', scatter_dimension=0, tiled=True)]
    all_gather x1 -> x0, waiting for transfers between devices: 25.8 us -> none  [per_device(): whole = lax.all_gather(draws, 'row', axis=0, tiled=True)]
    dynamic_slice x9 -> x0, local copies, waits for them, and re-layouts: 5.67 us -> none  [the longest x8 4.91 us: add_tile(): return lax.cond(flagged[row_pos, col_pos], dense, lambda acc: acc, total)]
    another operation x9 -> x0, loops' own time: 5.64 us -> none  [the longest x1 5.41 us: per_device(): lax.fori_loop(0, rows_local * cols_local, add_tile, partial_value)]
    unnamed x6 -> x17, local copies, waits for them, and re-layouts: 1.34 us -> 6.27 us
    all_gather x1 -> x0, local copies, waits for them, and re-layouts: 1.61 us -> none  [per_device(): whole = lax.all_gather(draws, 'row', axis=0, tiled=True)]
  transfers between devices with their start and end apart: 2 -> 0, of which waited for: 2 -> 0; matrix products, arithmetic and copies ran while one was open for 2% -> 0% of each run, Pallas kernels for 0% -> 0%
where the time goes in v1:
time: 45.5 us; the launch traced here: 45.3 us
  Pallas kernels  39 us (86%)
  local copies, waits for them, and re-layouts  6.27 us (14%)
    pallas_call x1, Pallas kernels, fused(): pl.pallas_call(functools.partial(kernel, cols), out_shape=jax.ShapeDtypeS...  39 us
    unnamed x17, local copies, waits for them, and re-layouts  6.27 us

profile of v1, /device:TPU:0, one launch (start us, length us, event | category | flops | bytes accessed | tf_op | source)
XLA Modules:
  0.0 45.3 jit_solution(16624196856588858409)
XLA Ops:
  0.0 0.0 copy-start.6
  0.0 2.1 %copy.8.u_hbm = bf16[2,4,1024,64]{3,2,1,0:T(8,128)(2,1)S(1)} copy(bf16[2,4,1024,64]{2,3,1,0:T(8,128)(2,1)} %param.8) | data formatting | bytes 2097152 | tf_op args[1]
  2.1 0.0 copy-done.6
  2.1 0.0 copy-start.1
  2.1 0.0 copy-start.2
  2.2 0.0 copy-start.3
  2.2 0.0 copy-start.4
  2.2 0.0 copy-start.5
  2.2 1.8 %copy.9.v_hbm = bf16[2,4,1024,64]{3,2,1,0:T(8,128)(2,1)} copy(bf16[2,4,1024,64]{2,3,1,0:T(8,128)(2,1)S(1)} %copy-done.6) | data formatting | bytes 2097152 | tf_op args[2]
  4.0 0.0 copy-done.1
  4.0 0.0 copy-done.2
  4.0 0.0 copy-done.3
  4.0 0.0 copy-done.4
  4.0 0.0 copy-done.5
  4.1 0.0 copy-start
  4.1 1.6 %copy-done = bf16[2,4,1024,64]{3,2,1,0:T(8,128)(2,1)S(1)} copy-done((bf16[2,4,1024,64]{3,2,1,0:T(8,128)(2,1)S(1)}, bf16[2,4,1024,64]{3,2,1,0:T(8,128)(2,1)}, u32[]{:S(2)}) %copy-start) | copy-done | bytes 1048600
  5.6 39.0 %shard_map.73 = f32[32,2048]{1,0:T(8,128)S(1)} custom-call(bf16[16,4096]{1,0:T(8,128)(2,1)S(1)} %copy-done.1, bf16[2,4,1024,64]{3,2,1,0:T(8,128)(2,1)S(1)} %copy.8.u_hbm, bf16[2,4,1024,64]{3,2,1,0:T(8,128)(2,1)S(1)} %copy-done, s32[2,4]{1,0:T(2,128)S(1)} %copy-done.4, s32[2,16]{1,0:T(2,128)S(1)} %copy-done.5, f32[2,2048]{1,0:T(2,128)S(1)} %copy-done.3, ...), custom_call_target="tpu_custom_call" | custom-call | flops 10000000000 | bytes 10000000 | tf_op jit(solution)/shard_map/pallas_call | solution.py:276
  44.6 0.7 %copy.11 = f32[32,2048]{1,0:T(8,128)} copy(f32[32,2048]{1,0:T(8,128)S(1)} %shard_map.73) | data formatting | bytes 524288
Async XLA Ops:
  0.0 2.1 %copy-start.6 = (bf16[2,4,1024,64]{2,3,1,0:T(8,128)(2,1)S(1)}, bf16[2,4,1024,64]{2,3,1,0:T(8,128)(2,1)}, u32[]{:S(2)}) copy-start(bf16[2,4,1024,64]{2,3,1,0:T(8,128)(2,1)} %param.9) | copy-start | bytes 3145732
  2.1 1.9 %copy-start.1 = (bf16[16,4096]{1,0:T(8,128)(2,1)S(1)}, bf16[16,4096]{1,0:T(8,128)(2,1)}, u32[]{:S(2)}) copy-start(bf16[16,4096]{1,0:T(8,128)(2,1)} %draws.1) | copy-start | bytes 393220
  2.1 1.9 %copy-start.2 = (f32[2,16384]{1,0:T(2,128)S(1)}, f32[2,16384]{1,0:T(2,128)}, u32[]{:S(2)}) copy-start(f32[2,16384]{1,0:T(2,128)} %col_coords.1) | copy-start | bytes 393220
  2.2 1.9 %copy-start.3 = (f32[2,2048]{1,0:T(2,128)S(1)}, f32[2,2048]{1,0:T(2,128)}, u32[]{:S(2)}) copy-start(f32[2,2048]{1,0:T(2,128)} %row_coords.1) | copy-start | bytes 49156
  2.2 1.9 %copy-start.4 = (s32[2,4]{1,0:T(2,128)S(1)}, s32[2,4]{1,0:T(2,128)}, u32[]{:S(2)}) copy-start(s32[2,4]{1,0:T(2,128)} %ranks.1) | copy-start | bytes 100
  2.2 1.9 %copy-start.5 = (s32[2,16]{1,0:T(2,128)S(1)}, s32[2,16]{1,0:T(2,128)}, u32[]{:S(2)}) copy-start(s32[2,16]{1,0:T(2,128)} %near.1) | copy-start | bytes 388
  4.1 1.6 %copy-start = (bf16[2,4,1024,64]{3,2,1,0:T(8,128)(2,1)S(1)}, bf16[2,4,1024,64]{3,2,1,0:T(8,128)(2,1)}, u32[]{:S(2)}) copy-start(bf16[2,4,1024,64]{3,2,1,0:T(8,128)(2,1)} %copy.9.v_hbm) | copy-start | bytes 3145732

commit v2 on v1

--- a/solution.py
+++ b/solution.py
@@ -11,7 +11,6 @@
 LOG2E = 1.4426950408889634
 TINY = 1e-12
 WIDE = 256
-TERMS = 32
 
 
 def matern_tile(col_part, row_part):
@@ -61,39 +60,13 @@
     return result
 
 
-def split3(value):
-    high = value.astype(jnp.bfloat16).astype(jnp.float32)
-    rest = value - high
-    middle = rest.astype(jnp.bfloat16).astype(jnp.float32)
-    return high, middle, rest - middle
-
-
-def write_terms(target, coords, is_row):
-    target[...] = jnp.zeros_like(target)
-    x = (coords[0:1, :] - 2.0) * LOG2E
-    y = (coords[1:2, :] - 2.0) * LOG2E
-    norm = split3(x * x + y * y)
-    at = 0
-    order = (0, 1, 0, 2, 0, 1) if is_row else (0, 0, 1, 0, 2, 1)
-    for value in (x, y):
-        parts = split3(value)
-        for piece in order:
-            target[at : at + 1, :] = parts[piece] * -2.0 if is_row else parts[piece]
-            at += 1
-    ones = jnp.ones_like(x)
-    for piece in range(3):
-        target[at : at + 1, :] = ones if is_row else norm[piece]
-        target[at + 3 : at + 4, :] = norm[piece] if is_row else ones
-        at += 1
-
-
 def kernel(
     cols, draws, u_hbm, v_hbm, ranks, near, row_coords, col_coords, out,
-    u, v, whole, dense, col_terms, col_left, row_terms, red, total, mail, inbox, own,
+    u, v, whole, dense, col_wide, row_terms, red, total, mail, inbox, own,
     factor_sem, gs_sem, gr_sem, ss_sem, sr_sem,
 ):
     groups, part_rows, width = whole.shape[0], whole.shape[1], whole.shape[2]
-    rows_local, cols_local, tile, rank = u.shape
+    rows_local, cols_local, rank, tile = u.shape
     nrhs = groups * part_rows
     share = nrhs // cols
     chunks = rows_local * tile // WIDE
@@ -121,11 +94,13 @@
     u_copy.start()
     v_copy.start()
 
-    write_terms(col_terms, col_coords[:, pl.ds(pl.multiple_of(first * tile, tile), width)], False)
-    write_terms(row_terms, row_coords[...], True)
-    for block in range(width // WIDE):
-        span = slice(block * WIDE, (block + 1) * WIDE)
-        col_left[span, :] = jnp.transpose(col_terms[:, span]).astype(jnp.bfloat16)
+    row_terms[...] = row_coords[...] * LOG2E
+    for block in range(width // 128):
+        at = pl.multiple_of(first * tile + block * 128, 128)
+        for axis in range(2):
+            line = col_coords[axis : axis + 1, pl.ds(at, 128)] * LOG2E
+            wide = jnp.transpose(jnp.broadcast_to(line, (128, 128)))
+            col_wide[axis, block * 128 : (block + 1) * 128, :] = wide
     whole[row] = draws[...]
     pl.semaphore_wait(barrier, 3 + cols)
 
@@ -140,13 +115,16 @@
         copy.start()
 
     def gen(chunk, j, quarter):
-        right = row_terms[:, chunk * WIDE : (chunk + 1) * WIDE].astype(jnp.bfloat16)
-        for half in range(2):
-            at = pl.multiple_of(j * tile + quarter * WIDE + half * 128, 128)
-            squared = jnp.dot(col_left[pl.ds(at, 128), :], right, preferred_element_type=jnp.float32)
-            squared = jnp.maximum(squared, TINY)
+        span = slice(chunk * WIDE, (chunk + 1) * WIDE)
+        row_x, row_y = row_terms[0:1, span], row_terms[1:2, span]
+        for part in range(4):
+            at = pl.multiple_of(j * tile + quarter * WIDE + part * 64, 64)
+            col_x, col_y = col_wide[0, pl.ds(at, 64), :], col_wide[1, pl.ds(at, 64), :]
+            delta_x = jnp.concatenate([col_x, col_x], axis=1) - row_x
+            delta_y = jnp.concatenate([col_y, col_y], axis=1) - row_y
+            squared = jnp.maximum(delta_x * delta_x + delta_y * delta_y, TINY)
             value = jnp.exp2(-(squared * lax.rsqrt(squared)))
-            dense[chunk, pl.ds(at, 128), :] = value.astype(jnp.bfloat16)
+            dense[chunk, pl.ds(at, 64), :] = value.astype(jnp.bfloat16)
 
     def flag(i, j):
         hit = jnp.where(near[i : i + 1, :] == first + j, 1.0, 0.0)
@@ -189,11 +167,8 @@
         i = chunk // per_row
         base = (chunk % per_row) * WIDE
         value = total[chunk % 2] * 0.03125
-        for j in range(cols_local):
-            value = value + lax.dot_general(
-                red[i, j], u[i, j, base : base + WIDE, :], (((1,), (1,)), ((), ())),
-                preferred_element_type=jnp.float32,
-            )
+        far = u[i, :, :, base : base + WIDE].reshape(cols_local * rank, WIDE)
+        value = value + jnp.dot(red[i], far, preferred_element_type=jnp.float32)
         value = value.reshape(cols, share, WIDE)
         mail[chunk] = value.astype(jnp.bfloat16)
         own[chunk] = value
@@ -227,10 +202,12 @@
             for j in range(cols_local):
                 left = whole[:, :, j * tile : (j + 1) * tile].reshape(nrhs, tile)
                 for i in range(rows_local):
-                    value = jnp.dot(left, v[i, j], preferred_element_type=jnp.float32)
+                    value = lax.dot_general(
+                        left, v[i, j], (((1,), (1,)), ((), ())), preferred_element_type=jnp.float32
+                    )
                     index = lax.broadcasted_iota(jnp.int32, value.shape, 1)
                     keep = jnp.where(index < ranks[i : i + 1, j : j + 1], 1.0, 0.0) * (1.0 - flag(i, j))
-                    red[i, j] = jnp.where(keep > 0.5, value, 0.0).astype(jnp.bfloat16)
+                    red[i, :, j * rank : (j + 1) * rank] = jnp.where(keep > 0.5, value, 0.0).astype(jnp.bfloat16)
         elif kind == "receive":
             for chunk in phase[1]:
                 receive(chunk)
@@ -279,14 +256,13 @@
         in_specs=[vmem, hbm, hbm, vmem, vmem, vmem, vmem],
         out_specs=vmem,
         scratch_shapes=[
-            pltpu.VMEM(u_factors.shape, jnp.bfloat16),
-            pltpu.VMEM(v_factors.shape, jnp.bfloat16),
+            pltpu.VMEM((rows_local, cols_local, rank, tile), jnp.bfloat16),
+            pltpu.VMEM((rows_local, cols_local, rank, tile), jnp.bfloat16),
             pltpu.VMEM((rows, part_rows, width), jnp.bfloat16),
             pltpu.VMEM((chunks, width, WIDE), jnp.bfloat16),
-            pltpu.VMEM((TERMS, width), jnp.float32),
-            pltpu.VMEM((width, TERMS), jnp.bfloat16),
-            pltpu.VMEM((TERMS, rows_local * tile), jnp.float32),
-            pltpu.VMEM((rows_local, cols_local, nrhs, rank), jnp.bfloat16),
+            pltpu.VMEM((2, width, 128), jnp.float32),
+            pltpu.VMEM((2, rows_local * tile), jnp.float32),
+            pltpu.VMEM((rows_local, nrhs, cols_local * rank), jnp.bfloat16),
             pltpu.VMEM((2, nrhs, WIDE), jnp.float32),
             pltpu.VMEM((chunks, cols, share, WIDE), jnp.bfloat16),
             pltpu.VMEM((chunks, cols - 1, share, WIDE), jnp.bfloat16),
@@ -301,7 +277,10 @@
             collective_id=0, has_side_effects=True, vmem_limit_bytes=48 * 1024 * 1024
         ),
         cost_estimate=pl.CostEstimate(flops=10**10, bytes_accessed=10**7, transcendentals=2 * 10**7),
-    )(draws, u_factors, v_factors, ranks, near, row_coords, col_coords)
+    )(
+        draws, jnp.swapaxes(u_factors, 2, 3), jnp.swapaxes(v_factors, 2, 3),
+        ranks, near, row_coords, col_coords,
+    )
 
 
 def solution(mesh):

time: 45.5 us -> 39.3 us (0.86)
  Pallas kernels: 39 us -> 32.6 us
    pallas_call x1, Pallas kernels: 39 us -> 32.6 us  [fused(): pl.pallas_call(functools.partial(kernel, cols), out_shape=jax.ShapeDtypeS...]
    unnamed x17 -> x15, local copies, waits for them, and re-layouts: 6.27 us -> 6.37 us
where the time goes in v2:
time: 39.3 us; the launch traced here: 39 us
  Pallas kernels  32.6 us (83%)
  local copies, waits for them, and re-layouts  6.37 us (16%)
    pallas_call x1, Pallas kernels, fused(): pl.pallas_call(functools.partial(kernel, cols), out_shape=jax.ShapeDtypeS...  32.6 us
    unnamed x15, local copies, waits for them, and re-layouts  6.37 us

profile of v2, /device:TPU:0, one launch (start us, length us, event | category | flops | bytes accessed | tf_op | source)
XLA Modules:
  0.0 39.0 jit_solution(203374381798360701)
XLA Ops:
  0.0 0.0 copy-start.6
  0.0 0.0 copy-start.5
  0.0 0.7 %copy-done.6 = s32[2,16]{1,0:T(2,128)S(1)} copy-done((s32[2,16]{1,0:T(2,128)S(1)}, s32[2,16]{1,0:T(2,128)}, u32[]{:S(2)}) %copy-start.6) | copy-done | bytes 152
  0.7 0.0 copy-done.5
  0.7 0.0 copy-start
  0.7 1.2 %copy-done = bf16[2,4,1024,64]{2,3,1,0:T(8,128)(2,1)S(1)} copy-done((bf16[2,4,1024,64]{2,3,1,0:T(8,128)(2,1)S(1)}, bf16[2,4,1024,64]{2,3,1,0:T(8,128)(2,1)}, u32[]{:S(2)}) %copy-start) | copy-done | bytes 1048600
  1.9 0.0 copy-start.1
  1.9 1.2 %copy-done.1 = bf16[2,4,1024,64]{2,3,1,0:T(8,128)(2,1)S(1)} copy-done((bf16[2,4,1024,64]{2,3,1,0:T(8,128)(2,1)S(1)}, bf16[2,4,1024,64]{2,3,1,0:T(8,128)(2,1)}, u32[]{:S(2)}) %copy-start.1) | copy-done | bytes 1048600
  3.1 0.0 copy-start.2
  3.1 0.9 %copy-done.2 = bf16[16,4096]{1,0:T(8,128)(2,1)S(1)} copy-done((bf16[16,4096]{1,0:T(8,128)(2,1)S(1)}, bf16[16,4096]{1,0:T(8,128)(2,1)}, u32[]{:S(2)}) %copy-start.2) | copy-done | bytes 131096
  4.1 0.0 copy-start.3
  4.1 0.9 %copy-done.3 = f32[2,16384]{1,0:T(2,128)S(1)} copy-done((f32[2,16384]{1,0:T(2,128)S(1)}, f32[2,16384]{1,0:T(2,128)}, u32[]{:S(2)}) %copy-start.3) | copy-done | bytes 131096
  5.0 0.0 copy-start.4
  5.0 0.7 %copy-done.4 = f32[2,2048]{1,0:T(2,128)S(1)} copy-done((f32[2,2048]{1,0:T(2,128)S(1)}, f32[2,2048]{1,0:T(2,128)}, u32[]{:S(2)}) %copy-start.4) | copy-done | bytes 16408
  5.7 32.6 %shard_map.73 = f32[32,2048]{1,0:T(8,128)S(1)} custom-call(bf16[16,4096]{1,0:T(8,128)(2,1)S(1)} %copy-done.2, bf16[2,4,64,1024]{3,2,1,0:T(8,128)(2,1)S(1)} %bitcast.2, bf16[2,4,64,1024]{3,2,1,0:T(8,128)(2,1)S(1)} %bitcast.3, s32[2,4]{1,0:T(2,128)S(1)} %copy-done.5, s32[2,16]{1,0:T(2,128)S(1)} %copy-done.6, f32[2,2048]{1,0:T(2,128)S(1)} %copy-done.4, ...), custom_call_target="tpu_custom_call" | custom-call | flops 10000000000 | bytes 10000000 | tf_op jit(solution)/shard_map/pallas_call | solution.py:253
  38.3 0.7 %copy.9 = f32[32,2048]{1,0:T(8,128)} copy(f32[32,2048]{1,0:T(8,128)S(1)} %shard_map.73) | data formatting | bytes 524288
Async XLA Ops:
  0.0 0.7 %copy-start.6 = (s32[2,16]{1,0:T(2,128)S(1)}, s32[2,16]{1,0:T(2,128)}, u32[]{:S(2)}) copy-start(s32[2,16]{1,0:T(2,128)} %near.1) | copy-start | bytes 388
  0.0 0.7 %copy-start.5 = (s32[2,4]{1,0:T(2,128)S(1)}, s32[2,4]{1,0:T(2,128)}, u32[]{:S(2)}) copy-start(s32[2,4]{1,0:T(2,128)} %ranks.1) | copy-start | bytes 100
  0.7 1.2 %copy-start = (bf16[2,4,1024,64]{2,3,1,0:T(8,128)(2,1)S(1)}, bf16[2,4,1024,64]{2,3,1,0:T(8,128)(2,1)}, u32[]{:S(2)}) copy-start(bf16[2,4,1024,64]{2,3,1,0:T(8,128)(2,1)} %param.8) | copy-start | bytes 3145732
  1.9 1.2 %copy-start.1 = (bf16[2,4,1024,64]{2,3,1,0:T(8,128)(2,1)S(1)}, bf16[2,4,1024,64]{2,3,1,0:T(8,128)(2,1)}, u32[]{:S(2)}) copy-start(bf16[2,4,1024,64]{2,3,1,0:T(8,128)(2,1)} %param.9) | copy-start | bytes 3145732
  3.1 0.9 %copy-start.2 = (bf16[16,4096]{1,0:T(8,128)(2,1)S(1)}, bf16[16,4096]{1,0:T(8,128)(2,1)}, u32[]{:S(2)}) copy-start(bf16[16,4096]{1,0:T(8,128)(2,1)} %draws.1) | copy-start | bytes 393220
  4.1 0.9 %copy-start.3 = (f32[2,16384]{1,0:T(2,128)S(1)}, f32[2,16384]{1,0:T(2,128)}, u32[]{:S(2)}) copy-start(f32[2,16384]{1,0:T(2,128)} %col_coords.1) | copy-start | bytes 393220
  5.0 0.7 %copy-start.4 = (f32[2,2048]{1,0:T(2,128)S(1)}, f32[2,2048]{1,0:T(2,128)}, u32[]{:S(2)}) copy-start(f32[2,2048]{1,0:T(2,128)} %row_coords.1) | copy-start | bytes 49156

commit v3 on v2

--- a/solution.py
+++ b/solution.py
@@ -61,8 +61,8 @@
 
 
 def kernel(
-    cols, draws, u_hbm, v_hbm, ranks, near, row_coords, col_coords, out,
-    u, v, whole, dense, col_wide, row_terms, red, total, mail, inbox, own,
+    cols, draws, u_hbm, v_hbm, ranks_hbm, near_hbm, row_hbm, col_hbm, out,
+    u, v, ranks, near, row_coords, col_coords, whole, dense, col_wide, row_terms, red_part, red, total, mail, inbox, own,
     factor_sem, gs_sem, gr_sem, ss_sem, sr_sem,
 ):
     groups, part_rows, width = whole.shape[0], whole.shape[1], whole.shape[2]
@@ -83,26 +83,32 @@
     def other(index):
         return index + 1 - 2 * (index % 2)
 
+    partner = col + 1 - 2 * (col % 2)
+    mirror = cols - 1 - col
+
     barrier = pltpu.get_barrier_semaphore()
     for peer in (sibling, beside, above, across):
         pl.semaphore_signal(barrier, inc=1, device_id=(peer, col), device_id_type=MESH)
-    for step in range(1, cols):
-        pl.semaphore_signal(barrier, inc=1, device_id=(row, (col + step) % cols), device_id_type=MESH)
-
-    u_copy = pltpu.make_async_copy(u_hbm, u, factor_sem.at[0])
-    v_copy = pltpu.make_async_copy(v_hbm, v, factor_sem.at[1])
-    u_copy.start()
-    v_copy.start()
-
+    for peer in (partner, mirror):
+        pl.semaphore_signal(barrier, inc=1, device_id=(row, peer), device_id_type=MESH)
+
+    span = pl.ds(pl.multiple_of(first * tile, tile), width)
+    pairs = (
+        (row_hbm, row_coords), (col_hbm.at[:, span], col_coords), (draws, whole.at[row]),
+        (near_hbm, near), (ranks_hbm, ranks), (u_hbm, u), (v_hbm, v),
+    )
+    fetches = [pltpu.make_async_copy(a, b, factor_sem.at[n]) for n, (a, b) in enumerate(pairs)]
+    for fetch in fetches:
+        fetch.start()
+    fetches[0].wait()
+    fetches[1].wait()
     row_terms[...] = row_coords[...] * LOG2E
     for block in range(width // 128):
-        at = pl.multiple_of(first * tile + block * 128, 128)
         for axis in range(2):
-            line = col_coords[axis : axis + 1, pl.ds(at, 128)] * LOG2E
+            line = col_coords[axis : axis + 1, block * 128 : (block + 1) * 128] * LOG2E
             wide = jnp.transpose(jnp.broadcast_to(line, (128, 128)))
             col_wide[axis, block * 128 : (block + 1) * 128, :] = wide
-    whole[row] = draws[...]
-    pl.semaphore_wait(barrier, 3 + cols)
+    pl.semaphore_wait(barrier, 6)
 
     def gather(source, slot, peer, index):
         return pltpu.make_async_remote_copy(
@@ -135,12 +141,26 @@
         left = whole[:, :, pl.ds(at, WIDE)].reshape(nrhs, WIDE)
         return jnp.dot(left, dense[chunk, pl.ds(at, WIDE), :], preferred_element_type=jnp.float32)
 
-    def step(makes, takes):
+    def reduce(j):
+        left = whole[:, :, pl.ds(pl.multiple_of(j * tile, tile), tile)].reshape(nrhs, tile)
+        for i in range(rows_local):
+            value = lax.dot_general(
+                left, v[i, j], (((1,), (1,)), ((), ())), preferred_element_type=jnp.float32
+            )
+            here = lax.broadcasted_iota(jnp.int32, (1, cols_local), 1) == j
+            most = jnp.sum(jnp.where(here, ranks[i : i + 1, :], 0), axis=1, keepdims=True)
+            index = lax.broadcasted_iota(jnp.int32, value.shape, 1)
+            keep = jnp.where(index < most, 1.0, 0.0) * (1.0 - flag(i, j))
+            red_part[i, j] = jnp.where(keep > 0.5, value, 0.0).astype(jnp.bfloat16)
+
+    def step(makes, takes, reduces=False):
         for take in takes:
             total[take % 2] = jnp.zeros_like(total[take % 2])
 
         def body(j, carry):
             sums = [None for _ in takes]
+            if reduces:
+                reduce(j)
             for quarter in range(tile // WIDE):
                 for make in makes:
                     gen(make, j, quarter)
@@ -152,15 +172,25 @@
             return carry
 
         lax.fori_loop(0, cols_local, body, 0)
+        if reduces:
+            for i in range(rows_local):
+                for j in range(cols_local):
+                    red[i, :, j * rank : (j + 1) * rank] = red_part[i, j]
         for take in takes:
             send(take)
 
-    def delivery(chunk, step):
-        peer = (col + step) % cols
+    def to_partner(chunk):
         return pltpu.make_async_remote_copy(
-            src_ref=mail.at[chunk, peer], dst_ref=inbox.at[chunk, step - 1],
-            send_sem=ss_sem.at[chunk, step - 1], recv_sem=sr_sem.at[chunk, step - 1],
-            device_id=(row, peer), device_id_type=MESH,
+            src_ref=mail.at[chunk, pl.ds(0, 2)], dst_ref=inbox.at[chunk, pl.ds(0, 2)],
+            send_sem=ss_sem.at[chunk, 0], recv_sem=sr_sem.at[chunk, 0],
+            device_id=(row, partner), device_id_type=MESH,
+        )
+
+    def to_mirror(chunk):
+        return pltpu.make_async_remote_copy(
+            src_ref=mail.at[chunk, 2], dst_ref=inbox.at[chunk, 2],
+            send_sem=ss_sem.at[chunk, 1], recv_sem=sr_sem.at[chunk, 1],
+            device_id=(row, mirror), device_id_type=MESH,
         )
 
     def send(chunk):
@@ -170,22 +200,26 @@
         far = u[i, :, :, base : base + WIDE].reshape(cols_local * rank, WIDE)
         value = value + jnp.dot(red[i], far, preferred_element_type=jnp.float32)
         value = value.reshape(cols, share, WIDE)
-        mail[chunk] = value.astype(jnp.bfloat16)
         own[chunk] = value
-        for step in range(1, cols):
-            delivery(chunk, step).start()
+        mail[chunk, 0] = own[chunk, partner].astype(jnp.bfloat16)
+        mail[chunk, 1] = own[chunk, cols - 1 - partner].astype(jnp.bfloat16)
+        to_partner(chunk).start()
+
+    def relay(chunk):
+        to_partner(chunk).wait_recv()
+        passed = own[chunk, mirror] + inbox[chunk, 1].astype(jnp.float32)
+        mail[chunk, 2] = passed.astype(jnp.bfloat16)
+        to_mirror(chunk).start()
 
     def receive(chunk):
-        value = own[chunk, col]
-        for step in range(1, cols):
-            delivery(chunk, step).wait_recv()
-            value = value + inbox[chunk, step - 1].astype(jnp.float32)
-        out[:, chunk * WIDE : (chunk + 1) * WIDE] = value
+        to_mirror(chunk).wait_recv()
+        value = own[chunk, col] + inbox[chunk, 0].astype(jnp.float32)
+        out[:, chunk * WIDE : (chunk + 1) * WIDE] = value + inbox[chunk, 2].astype(jnp.float32)
 
     for phase in PLAN:
         kind = phase[0]
         if kind == "step":
-            step(phase[1], phase[2])
+            step(*phase[1:])
         elif kind == "forward":
             for index in phase[1]:
                 firsts[index].wait_recv()
@@ -196,18 +230,11 @@
                 slot = other((beside, above, across)[index])
                 gather(whole.at[slot], slot, sibling, 4 + index).wait_recv()
             firsts[3].wait_recv()
-        elif kind == "reduce":
-            u_copy.wait()
-            v_copy.wait()
-            for j in range(cols_local):
-                left = whole[:, :, j * tile : (j + 1) * tile].reshape(nrhs, tile)
-                for i in range(rows_local):
-                    value = lax.dot_general(
-                        left, v[i, j], (((1,), (1,)), ((), ())), preferred_element_type=jnp.float32
-                    )
-                    index = lax.broadcasted_iota(jnp.int32, value.shape, 1)
-                    keep = jnp.where(index < ranks[i : i + 1, j : j + 1], 1.0, 0.0) * (1.0 - flag(i, j))
-                    red[i, :, j * rank : (j + 1) * rank] = jnp.where(keep > 0.5, value, 0.0).astype(jnp.bfloat16)
+            for fetch in fetches[2:]:
+                fetch.wait()
+        elif kind == "relay":
+            for chunk in phase[1]:
+                relay(chunk)
         elif kind == "receive":
             for chunk in phase[1]:
                 receive(chunk)
@@ -218,8 +245,8 @@
         slot = (beside, above, across)[index]
         gather(whole.at[slot], slot, sibling, 4 + index).wait_send()
     for chunk in range(chunks):
-        for step_at in range(1, cols):
-            delivery(chunk, step_at).wait_send()
+        to_partner(chunk).wait_send()
+        to_mirror(chunk).wait_send()
 
 
 PLAN = (
@@ -228,17 +255,25 @@
     ("forward", (0, 1)),
     ("step", (2,), ()),
     ("forward", (2,)),
-    ("step", (3,), ()),
     ("ready",),
-    ("reduce",),
-    ("step", (4,), (0, 1)),
-    ("step", (5,), (2, 3)),
-    ("step", (6,), (4, 5)),
-    ("receive", (0, 1)),
+    ("step", (), (0,), True),
+    ("step", (3,), (1, 2)),
+    ("relay", (0,)),
+    ("step", (4,), (3,)),
+    ("relay", (1, 2)),
+    ("receive", (0,)),
+    ("step", (5,), (4,)),
+    ("relay", (3,)),
+    ("receive", (1, 2)),
+    ("step", (6,), (5,)),
+    ("relay", (4,)),
+    ("receive", (3,)),
     ("step", (7,), (6,)),
-    ("receive", (2, 3)),
+    ("relay", (5,)),
+    ("receive", (4,)),
     ("step", (), (7,)),
-    ("receive", (4, 5, 6, 7)),
+    ("relay", (6, 7)),
+    ("receive", (5, 6, 7)),
 )
 
 
@@ -253,28 +288,33 @@
     return pl.pallas_call(
         functools.partial(kernel, cols),
         out_shape=jax.ShapeDtypeStruct((share, rows_local * tile), jnp.float32),
-        in_specs=[vmem, hbm, hbm, vmem, vmem, vmem, vmem],
+        in_specs=[hbm] * 7,
         out_specs=vmem,
         scratch_shapes=[
             pltpu.VMEM((rows_local, cols_local, rank, tile), jnp.bfloat16),
             pltpu.VMEM((rows_local, cols_local, rank, tile), jnp.bfloat16),
+            pltpu.VMEM(ranks.shape, jnp.int32),
+            pltpu.VMEM(near.shape, jnp.int32),
+            pltpu.VMEM(row_coords.shape, jnp.float32),
+            pltpu.VMEM((2, width), jnp.float32),
             pltpu.VMEM((rows, part_rows, width), jnp.bfloat16),
             pltpu.VMEM((chunks, width, WIDE), jnp.bfloat16),
             pltpu.VMEM((2, width, 128), jnp.float32),
             pltpu.VMEM((2, rows_local * tile), jnp.float32),
+            pltpu.VMEM((rows_local, cols_local, nrhs, rank), jnp.bfloat16),
             pltpu.VMEM((rows_local, nrhs, cols_local * rank), jnp.bfloat16),
             pltpu.VMEM((2, nrhs, WIDE), jnp.float32),
-            pltpu.VMEM((chunks, cols, share, WIDE), jnp.bfloat16),
-            pltpu.VMEM((chunks, cols - 1, share, WIDE), jnp.bfloat16),
+            pltpu.VMEM((chunks, 3, share, WIDE), jnp.bfloat16),
+            pltpu.VMEM((chunks, 3, share, WIDE), jnp.bfloat16),
             pltpu.VMEM((chunks, cols, share, WIDE), jnp.float32),
-            pltpu.SemaphoreType.DMA((2,)),
             pltpu.SemaphoreType.DMA((7,)),
             pltpu.SemaphoreType.DMA((7,)),
-            pltpu.SemaphoreType.DMA((chunks, cols - 1)),
-            pltpu.SemaphoreType.DMA((chunks, cols - 1)),
+            pltpu.SemaphoreType.DMA((7,)),
+            pltpu.SemaphoreType.DMA((chunks, 2)),
+            pltpu.SemaphoreType.DMA((chunks, 2)),
         ],
         compiler_params=pltpu.CompilerParams(
-            collective_id=0, has_side_effects=True, vmem_limit_bytes=48 * 1024 * 1024
+            collective_id=0, has_side_effects=True, vmem_limit_bytes=60 * 1024 * 1024
         ),
         cost_estimate=pl.CostEstimate(flops=10**10, bytes_accessed=10**7, transcendentals=2 * 10**7),
     )(

time: 39.3 us -> 42.9 us (1.092)
  Pallas kernels: 32.6 us -> 41 us
  local copies, waits for them, and re-layouts: 6.37 us -> 1.67 us
    pallas_call x1, Pallas kernels: 32.6 us -> 41 us  [fused(): pl.pallas_call(functools.partial(kernel, cols), out_shape=jax.ShapeDtypeS...]
    unnamed x15 -> x1, local copies, waits for them, and re-layouts: 6.37 us -> 1.67 us
where the time goes in v3:
time: 42.9 us; the launch traced here: 42.7 us
  Pallas kernels  41 us (96%)
  local copies, waits for them, and re-layouts  1.67 us (4%)
    pallas_call x1, Pallas kernels, fused(): pl.pallas_call(functools.partial(kernel, cols), out_shape=jax.ShapeDtypeS...  41 us
    unnamed x1, local copies, waits for them, and re-layouts  1.67 us

profile of v3, /device:TPU:0, one launch (start us, length us, event | category | flops | bytes accessed | tf_op | source)
XLA Modules:
  0.0 42.7 jit_solution(16939712006057971226)
XLA Ops:
  0.0 41.0 %shard_map.73 = f32[32,2048]{1,0:T(8,128)} custom-call(bf16[16,4096]{1,0:T(8,128)(2,1)} %draws.1, bf16[2,4,64,1024]{3,2,1,0:T(8,128)(2,1)} %bitcast.2, bf16[2,4,64,1024]{3,2,1,0:T(8,128)(2,1)} %bitcast.3, s32[2,4]{1,0:T(2,128)} %ranks_hbm.1, s32[2,16]{1,0:T(2,128)} %near_hbm.1, f32[2,2048]{1,0:T(2,128)} %row_hbm.1, f32[2,16384]{1,0:T(2,128)} %col_hbm.1), custom_call_target="tpu_custom_call" | custom-call | flops 10000000000 | bytes 10000000 | tf_op jit(solution)/shard_map/pallas_call | solution.py:288
  41.0 1.7 %copy.9 = f32[32,2048]{1,0:T(8,128)} copy(f32[32,2048]{1,0:T(8,128)} %shard_map.73) | data formatting | bytes 524288

commit v4 on v2

--- a/solution.py
+++ b/solution.py
@@ -60,9 +60,16 @@
     return result
 
 
+def split3(value):
+    high = value.astype(jnp.bfloat16).astype(jnp.float32)
+    rest = value - high
+    middle = rest.astype(jnp.bfloat16).astype(jnp.float32)
+    return high, middle, rest - middle
+
+
 def kernel(
-    cols, draws, u_hbm, v_hbm, ranks, near, row_coords, col_coords, out,
-    u, v, whole, dense, col_wide, row_terms, red, total, mail, inbox, own,
+    cols, draws, u_hbm, v_hbm, ranks_hbm, near_hbm, row_hbm, col_hbm, out,
+    u, v, ranks, near, row_coords, col_coords, whole, dense, terms, col_wide, row_terms, red_part, red, total, mail, inbox, own,
     factor_sem, gs_sem, gr_sem, ss_sem, sr_sem,
 ):
     groups, part_rows, width = whole.shape[0], whole.shape[1], whole.shape[2]
@@ -86,22 +93,36 @@
     barrier = pltpu.get_barrier_semaphore()
     for peer in (sibling, beside, above, across):
         pl.semaphore_signal(barrier, inc=1, device_id=(peer, col), device_id_type=MESH)
-    for step in range(1, cols):
-        pl.semaphore_signal(barrier, inc=1, device_id=(row, (col + step) % cols), device_id_type=MESH)
-
-    u_copy = pltpu.make_async_copy(u_hbm, u, factor_sem.at[0])
-    v_copy = pltpu.make_async_copy(v_hbm, v, factor_sem.at[1])
-    u_copy.start()
-    v_copy.start()
-
+    for hop in range(1, cols):
+        pl.semaphore_signal(barrier, inc=1, device_id=(row, (col + hop) % cols), device_id_type=MESH)
+
+    span = pl.ds(pl.multiple_of(first * tile, tile), width)
+    pairs = (
+        (row_hbm, row_coords), (col_hbm.at[:, span], col_coords), (draws, whole.at[row]),
+        (near_hbm, near), (ranks_hbm, ranks), (u_hbm, u), (v_hbm, v),
+    )
+    fetches = [pltpu.make_async_copy(a, b, factor_sem.at[n]) for n, (a, b) in enumerate(pairs)]
+    for fetch in fetches:
+        fetch.start()
+    fetches[0].wait()
+    fetches[1].wait()
     row_terms[...] = row_coords[...] * LOG2E
-    for block in range(width // 128):
-        at = pl.multiple_of(first * tile + block * 128, 128)
-        for axis in range(2):
-            line = col_coords[axis : axis + 1, pl.ds(at, 128)] * LOG2E
-            wide = jnp.transpose(jnp.broadcast_to(line, (128, 128)))
-            col_wide[axis, block * 128 : (block + 1) * 128, :] = wide
-    whole[row] = draws[...]
+    terms[...] = jnp.zeros_like(terms)
+    line = lax.broadcasted_iota(jnp.int32, (16, 256), 0)
+    lane = lax.broadcasted_iota(jnp.int32, (16, 256), 1)
+    ones = jnp.where((line < 6) & ((line < 3) == (lane < 128)), 1.0, 0.0).astype(jnp.bfloat16)
+    for axis in range(2):
+        parts = split3(col_coords[axis : axis + 1, :] * LOG2E)
+        for piece in range(3):
+            terms[3 * axis + piece : 3 * axis + piece + 1, :] = parts[piece]
+    for block in range(width // 512):
+        at = slice(block * 512, (block + 1) * 512)
+        wide = lax.dot_general(
+            terms[:, at].astype(jnp.bfloat16), ones, (((0,), (0,)), ((), ())),
+            preferred_element_type=jnp.float32,
+        )
+        col_wide[0, at, :] = wide[:, :128]
+        col_wide[1, at, :] = wide[:, 128:]
     pl.semaphore_wait(barrier, 3 + cols)
 
     def gather(source, slot, peer, index):
@@ -124,34 +145,49 @@
             delta_y = jnp.concatenate([col_y, col_y], axis=1) - row_y
             squared = jnp.maximum(delta_x * delta_x + delta_y * delta_y, TINY)
             value = jnp.exp2(-(squared * lax.rsqrt(squared)))
-            dense[chunk, pl.ds(at, 64), :] = value.astype(jnp.bfloat16)
+            dense[chunk][pl.ds(at, 64), :] = value.astype(jnp.bfloat16)
 
     def flag(i, j):
         hit = jnp.where(near[i : i + 1, :] == first + j, 1.0, 0.0)
         return jnp.max(hit, axis=1, keepdims=True)
 
-    def mul(chunk, j, quarter):
-        at = pl.multiple_of(j * tile + quarter * WIDE, WIDE)
-        left = whole[:, :, pl.ds(at, WIDE)].reshape(nrhs, WIDE)
-        return jnp.dot(left, dense[chunk, pl.ds(at, WIDE), :], preferred_element_type=jnp.float32)
-
-    def step(makes, takes):
+    def mul(chunk, j):
+        span = pl.ds(pl.multiple_of(j * tile, tile), tile)
+        left = whole[:, :, span].reshape(nrhs, tile)
+        return jnp.dot(left, dense[chunk][span, :], preferred_element_type=jnp.float32)
+
+    def reduce(j):
+        left = whole[:, :, pl.ds(pl.multiple_of(j * tile, tile), tile)].reshape(nrhs, tile)
+        for i in range(rows_local):
+            value = lax.dot_general(
+                left, v[i, j], (((1,), (1,)), ((), ())), preferred_element_type=jnp.float32
+            )
+            here = lax.broadcasted_iota(jnp.int32, (1, cols_local), 1) == j
+            most = jnp.sum(jnp.where(here, ranks[i : i + 1, :], 0), axis=1, keepdims=True)
+            index = lax.broadcasted_iota(jnp.int32, value.shape, 1)
+            keep = jnp.where(index < most, 1.0, 0.0) * (1.0 - flag(i, j))
+            red_part[i, j] = jnp.where(keep > 0.5, value, 0.0).astype(jnp.bfloat16)
+
+    def step(makes, takes, reduces=False):
         for take in takes:
             total[take % 2] = jnp.zeros_like(total[take % 2])
 
         def body(j, carry):
-            sums = [None for _ in takes]
+            if reduces:
+                reduce(j)
+            sums = [mul(take, j) for take in takes]
             for quarter in range(tile // WIDE):
                 for make in makes:
                     gen(make, j, quarter)
-                for n, take in enumerate(takes):
-                    product = mul(take, j, quarter)
-                    sums[n] = product if sums[n] is None else sums[n] + product
             for n, take in enumerate(takes):
                 total[take % 2] += sums[n] * flag(take // per_row, j)
             return carry
 
         lax.fori_loop(0, cols_local, body, 0)
+        if reduces:
+            for i in range(rows_local):
+                for j in range(cols_local):
+                    red[i, :, j * rank : (j + 1) * rank] = red_part[i, j]
         for take in takes:
             send(take)
 
@@ -185,7 +221,7 @@
     for phase in PLAN:
         kind = phase[0]
         if kind == "step":
-            step(phase[1], phase[2])
+            step(*phase[1:])
         elif kind == "forward":
             for index in phase[1]:
                 firsts[index].wait_recv()
@@ -196,18 +232,8 @@
                 slot = other((beside, above, across)[index])
                 gather(whole.at[slot], slot, sibling, 4 + index).wait_recv()
             firsts[3].wait_recv()
-        elif kind == "reduce":
-            u_copy.wait()
-            v_copy.wait()
-            for j in range(cols_local):
-                left = whole[:, :, j * tile : (j + 1) * tile].reshape(nrhs, tile)
-                for i in range(rows_local):
-                    value = lax.dot_general(
-                        left, v[i, j], (((1,), (1,)), ((), ())), preferred_element_type=jnp.float32
-                    )
-                    index = lax.broadcasted_iota(jnp.int32, value.shape, 1)
-                    keep = jnp.where(index < ranks[i : i + 1, j : j + 1], 1.0, 0.0) * (1.0 - flag(i, j))
-                    red[i, :, j * rank : (j + 1) * rank] = jnp.where(keep > 0.5, value, 0.0).astype(jnp.bfloat16)
+            for fetch in fetches[2:]:
+                fetch.wait()
         elif kind == "receive":
             for chunk in phase[1]:
                 receive(chunk)
@@ -230,8 +256,7 @@
     ("forward", (2,)),
     ("step", (3,), ()),
     ("ready",),
-    ("reduce",),
-    ("step", (4,), (0, 1)),
+    ("step", (4,), (0, 1), True),
     ("step", (5,), (2, 3)),
     ("step", (6,), (4, 5)),
     ("receive", (0, 1)),
@@ -253,28 +278,34 @@
     return pl.pallas_call(
         functools.partial(kernel, cols),
         out_shape=jax.ShapeDtypeStruct((share, rows_local * tile), jnp.float32),
-        in_specs=[vmem, hbm, hbm, vmem, vmem, vmem, vmem],
+        in_specs=[hbm] * 7,
         out_specs=vmem,
         scratch_shapes=[
             pltpu.VMEM((rows_local, cols_local, rank, tile), jnp.bfloat16),
             pltpu.VMEM((rows_local, cols_local, rank, tile), jnp.bfloat16),
+            pltpu.VMEM(ranks.shape, jnp.int32),
+            pltpu.VMEM(near.shape, jnp.int32),
+            pltpu.VMEM(row_coords.shape, jnp.float32),
+            pltpu.VMEM((2, width), jnp.float32),
             pltpu.VMEM((rows, part_rows, width), jnp.bfloat16),
-            pltpu.VMEM((chunks, width, WIDE), jnp.bfloat16),
+            [pltpu.VMEM((width, WIDE), jnp.bfloat16) for _ in range(chunks)],
+            pltpu.VMEM((16, width), jnp.float32),
             pltpu.VMEM((2, width, 128), jnp.float32),
             pltpu.VMEM((2, rows_local * tile), jnp.float32),
+            pltpu.VMEM((rows_local, cols_local, nrhs, rank), jnp.bfloat16),
             pltpu.VMEM((rows_local, nrhs, cols_local * rank), jnp.bfloat16),
             pltpu.VMEM((2, nrhs, WIDE), jnp.float32),
             pltpu.VMEM((chunks, cols, share, WIDE), jnp.bfloat16),
             pltpu.VMEM((chunks, cols - 1, share, WIDE), jnp.bfloat16),
             pltpu.VMEM((chunks, cols, share, WIDE), jnp.float32),
-            pltpu.SemaphoreType.DMA((2,)),
+            pltpu.SemaphoreType.DMA((7,)),
             pltpu.SemaphoreType.DMA((7,)),
             pltpu.SemaphoreType.DMA((7,)),
             pltpu.SemaphoreType.DMA((chunks, cols - 1)),
             pltpu.SemaphoreType.DMA((chunks, cols - 1)),
         ],
         compiler_params=pltpu.CompilerParams(
-            collective_id=0, has_side_effects=True, vmem_limit_bytes=48 * 1024 * 1024
+            collective_id=0, has_side_effects=True, vmem_limit_bytes=60 * 1024 * 1024
         ),
         cost_estimate=pl.CostEstimate(flops=10**10, bytes_accessed=10**7, transcendentals=2 * 10**7),
     )(

time: 39.3 us -> 35.3 us (0.90)
  local copies, waits for them, and re-layouts: 6.37 us -> 1.67 us
  Pallas kernels: 32.6 us -> 33.4 us
    unnamed x15 -> x1, local copies, waits for them, and re-layouts: 6.37 us -> 1.67 us
    pallas_call x1, Pallas kernels: 32.6 us -> 33.4 us  [fused(): pl.pallas_call(functools.partial(kernel, cols), out_shape=jax.ShapeDtypeS...]
where the time goes in v4:
time: 35.3 us; the launch traced here: 35.1 us
  Pallas kernels  33.4 us (95%)
  local copies, waits for them, and re-layouts  1.67 us (5%)
    pallas_call x1, Pallas kernels, fused(): pl.pallas_call(functools.partial(kernel, cols), out_shape=jax.ShapeDtypeS...  33.4 us
    unnamed x1, local copies, waits for them, and re-layouts  1.67 us

profile of v4, /device:TPU:0, one launch (start us, length us, event | category | flops | bytes accessed | tf_op | source)
XLA Modules:
  0.0 35.1 jit_solution(14108779228106258061)
XLA Ops:
  0.0 33.4 %shard_map.73 = f32[32,2048]{1,0:T(8,128)} custom-call(bf16[16,4096]{1,0:T(8,128)(2,1)} %draws.1, bf16[2,4,64,1024]{3,2,1,0:T(8,128)(2,1)} %bitcast.2, bf16[2,4,64,1024]{3,2,1,0:T(8,128)(2,1)} %bitcast.3, s32[2,4]{1,0:T(2,128)} %ranks_hbm.1, s32[2,16]{1,0:T(2,128)} %near_hbm.1, f32[2,2048]{1,0:T(2,128)} %row_hbm.1, f32[2,16384]{1,0:T(2,128)} %col_hbm.1), custom_call_target="tpu_custom_call" | custom-call | flops 10000000000 | bytes 10000000 | tf_op jit(solution)/shard_map/pallas_call | solution.py:278
  33.4 1.7 %copy.9 = f32[32,2048]{1,0:T(8,128)} copy(f32[32,2048]{1,0:T(8,128)} %shard_map.73) | data formatting | bytes 524288

commit v5 on v3

--- a/solution.py
+++ b/solution.py
@@ -60,9 +60,16 @@
     return result
 
 
+def split3(value):
+    high = value.astype(jnp.bfloat16).astype(jnp.float32)
+    rest = value - high
+    middle = rest.astype(jnp.bfloat16).astype(jnp.float32)
+    return high, middle, rest - middle
+
+
 def kernel(
     cols, draws, u_hbm, v_hbm, ranks_hbm, near_hbm, row_hbm, col_hbm, out,
-    u, v, ranks, near, row_coords, col_coords, whole, dense, col_wide, row_terms, red_part, red, total, mail, inbox, own,
+    u, v, ranks, near, row_coords, col_coords, whole, dense, terms, col_wide, row_terms, red_part, red, total, mail, inbox, own,
     factor_sem, gs_sem, gr_sem, ss_sem, sr_sem,
 ):
     groups, part_rows, width = whole.shape[0], whole.shape[1], whole.shape[2]
@@ -80,14 +87,11 @@
     above = row + 4 - 8 * ((row // 4) % 2)
     across = beside + 4 - 8 * ((row // 4) % 2)
 
-    def other(index):
-        return index + 1 - 2 * (index % 2)
-
     partner = col + 1 - 2 * (col % 2)
     mirror = cols - 1 - col
 
     barrier = pltpu.get_barrier_semaphore()
-    for peer in (sibling, beside, above, across):
+    for peer in (sibling, beside, above):
         pl.semaphore_signal(barrier, inc=1, device_id=(peer, col), device_id_type=MESH)
     for peer in (partner, mirror):
         pl.semaphore_signal(barrier, inc=1, device_id=(row, peer), device_id_type=MESH)
@@ -103,20 +107,45 @@
     fetches[0].wait()
     fetches[1].wait()
     row_terms[...] = row_coords[...] * LOG2E
-    for block in range(width // 128):
-        for axis in range(2):
-            line = col_coords[axis : axis + 1, block * 128 : (block + 1) * 128] * LOG2E
-            wide = jnp.transpose(jnp.broadcast_to(line, (128, 128)))
-            col_wide[axis, block * 128 : (block + 1) * 128, :] = wide
-    pl.semaphore_wait(barrier, 6)
-
-    def gather(source, slot, peer, index):
+    terms[...] = jnp.zeros_like(terms)
+    line = lax.broadcasted_iota(jnp.int32, (16, 256), 0)
+    lane = lax.broadcasted_iota(jnp.int32, (16, 256), 1)
+    ones = jnp.where((line < 6) & ((line < 3) == (lane < 128)), 1.0, 0.0).astype(jnp.bfloat16)
+    for axis in range(2):
+        parts = split3(col_coords[axis : axis + 1, :] * LOG2E)
+        for piece in range(3):
+            terms[3 * axis + piece : 3 * axis + piece + 1, :] = parts[piece]
+    for block in range(width // 512):
+        at = slice(block * 512, (block + 1) * 512)
+        wide = lax.dot_general(
+            terms[:, at].astype(jnp.bfloat16), ones, (((0,), (0,)), ((), ())),
+            preferred_element_type=jnp.float32,
+        )
+        col_wide[0, at, :] = wide[:, :128]
+        col_wide[1, at, :] = wide[:, 128:]
+    pl.semaphore_wait(barrier, 5)
+
+    def gather(source, target, peer, index):
         return pltpu.make_async_remote_copy(
-            src_ref=source, dst_ref=whole.at[slot], send_sem=gs_sem.at[index],
+            src_ref=source, dst_ref=target, send_sem=gs_sem.at[index],
             recv_sem=gr_sem.at[index], device_id=(peer, col), device_id_type=MESH,
         )
 
-    firsts = [gather(draws, row, peer, index) for index, peer in enumerate((beside, above, across, sibling))]
+    def half(slot, which):
+        return whole.at[slot, :, pl.ds(which * (width // 2), width // 2)]
+
+    def hop(which):
+        slot, peer = ((beside, above), (above, beside))[which]
+        return gather(half(slot, which), half(slot, which), peer, 2 + 5 * which)
+
+    def pass_on(index):
+        slot = (beside, above, across)[index]
+        return gather(whole.at[slot], whole.at[slot], sibling, 4 + index)
+
+    firsts = [
+        gather(draws, whole.at[row], peer, index)
+        for peer, index in ((beside, 0), (above, 1), (sibling, 3))
+    ]
     for copy in firsts:
         copy.start()
 
@@ -130,16 +159,16 @@
             delta_y = jnp.concatenate([col_y, col_y], axis=1) - row_y
             squared = jnp.maximum(delta_x * delta_x + delta_y * delta_y, TINY)
             value = jnp.exp2(-(squared * lax.rsqrt(squared)))
-            dense[chunk, pl.ds(at, 64), :] = value.astype(jnp.bfloat16)
+            dense[chunk][pl.ds(at, 64), :] = value.astype(jnp.bfloat16)
 
     def flag(i, j):
         hit = jnp.where(near[i : i + 1, :] == first + j, 1.0, 0.0)
         return jnp.max(hit, axis=1, keepdims=True)
 
-    def mul(chunk, j, quarter):
-        at = pl.multiple_of(j * tile + quarter * WIDE, WIDE)
-        left = whole[:, :, pl.ds(at, WIDE)].reshape(nrhs, WIDE)
-        return jnp.dot(left, dense[chunk, pl.ds(at, WIDE), :], preferred_element_type=jnp.float32)
+    def mul(chunk, j):
+        span = pl.ds(pl.multiple_of(j * tile, tile), tile)
+        left = whole[:, :, span].reshape(nrhs, tile)
+        return jnp.dot(left, dense[chunk][span, :], preferred_element_type=jnp.float32)
 
     def reduce(j):
         left = whole[:, :, pl.ds(pl.multiple_of(j * tile, tile), tile)].reshape(nrhs, tile)
@@ -158,15 +187,12 @@
             total[take % 2] = jnp.zeros_like(total[take % 2])
 
         def body(j, carry):
-            sums = [None for _ in takes]
             if reduces:
                 reduce(j)
+            sums = [mul(take, j) for take in takes]
             for quarter in range(tile // WIDE):
                 for make in makes:
                     gen(make, j, quarter)
-                for n, take in enumerate(takes):
-                    product = mul(take, j, quarter)
-                    sums[n] = product if sums[n] is None else sums[n] + product
             for n, take in enumerate(takes):
                 total[take % 2] += sums[n] * flag(take // per_row, j)
             return carry
@@ -221,15 +247,18 @@
         if kind == "step":
             step(*phase[1:])
         elif kind == "forward":
-            for index in phase[1]:
+            for index in range(2):
                 firsts[index].wait_recv()
-                slot = (beside, above, across)[index]
-                gather(whole.at[slot], slot, sibling, 4 + index).start()
+                hop(index).start()
+                pass_on(index).start()
+        elif kind == "corner":
+            for which in range(2):
+                hop(which).wait_recv()
+            pass_on(2).start()
         elif kind == "ready":
             for index in range(3):
-                slot = other((beside, above, across)[index])
-                gather(whole.at[slot], slot, sibling, 4 + index).wait_recv()
-            firsts[3].wait_recv()
+                pass_on(index).wait_recv()
+            firsts[2].wait_recv()
             for fetch in fetches[2:]:
                 fetch.wait()
         elif kind == "relay":
@@ -241,9 +270,10 @@
 
     for copy in firsts:
         copy.wait_send()
+    for which in range(2):
+        hop(which).wait_send()
     for index in range(3):
-        slot = (beside, above, across)[index]
-        gather(whole.at[slot], slot, sibling, 4 + index).wait_send()
+        pass_on(index).wait_send()
     for chunk in range(chunks):
         to_partner(chunk).wait_send()
         to_mirror(chunk).wait_send()
@@ -252,28 +282,25 @@
 PLAN = (
     ("step", (0,), ()),
     ("step", (1,), ()),
-    ("forward", (0, 1)),
+    ("forward",),
     ("step", (2,), ()),
-    ("forward", (2,)),
+    ("corner",),
     ("ready",),
-    ("step", (), (0,), True),
-    ("step", (3,), (1, 2)),
-    ("relay", (0,)),
+    ("step", (), (0, 1), True),
+    ("step", (3,), (2,)),
     ("step", (4,), (3,)),
-    ("relay", (1, 2)),
-    ("receive", (0,)),
+    ("relay", (0, 1)),
     ("step", (5,), (4,)),
+    ("relay", (2,)),
+    ("step", (6,), (5,)),
     ("relay", (3,)),
-    ("receive", (1, 2)),
-    ("step", (6,), (5,)),
-    ("relay", (4,)),
-    ("receive", (3,)),
+    ("receive", (0, 1)),
     ("step", (7,), (6,)),
-    ("relay", (5,)),
-    ("receive", (4,)),
+    ("relay", (4, 5)),
     ("step", (), (7,)),
+    ("receive", (2, 3)),
     ("relay", (6, 7)),
-    ("receive", (5, 6, 7)),
+    ("receive", (4, 5, 6, 7)),
 )
 
 
@@ -298,7 +325,8 @@
             pltpu.VMEM(row_coords.shape, jnp.float32),
             pltpu.VMEM((2, width), jnp.float32),
             pltpu.VMEM((rows, part_rows, width), jnp.bfloat16),
-            pltpu.VMEM((chunks, width, WIDE), jnp.bfloat16),
+            [pltpu.VMEM((width, WIDE), jnp.bfloat16) for _ in range(chunks)],
+            pltpu.VMEM((16, width), jnp.float32),
             pltpu.VMEM((2, width, 128), jnp.float32),
             pltpu.VMEM((2, rows_local * tile), jnp.float32),
             pltpu.VMEM((rows_local, cols_local, nrhs, rank), jnp.bfloat16),
@@ -308,8 +336,8 @@
             pltpu.VMEM((chunks, 3, share, WIDE), jnp.bfloat16),
             pltpu.VMEM((chunks, cols, share, WIDE), jnp.float32),
             pltpu.SemaphoreType.DMA((7,)),
-            pltpu.SemaphoreType.DMA((7,)),
-            pltpu.SemaphoreType.DMA((7,)),
+            pltpu.SemaphoreType.DMA((8,)),
+            pltpu.SemaphoreType.DMA((8,)),
             pltpu.SemaphoreType.DMA((chunks, 2)),
             pltpu.SemaphoreType.DMA((chunks, 2)),
         ],

time: 42.9 us -> 40.3 us (0.939)
  Pallas kernels: 41 us -> 38.4 us
    pallas_call x1, Pallas kernels: 41 us -> 38.4 us  [fused(): pl.pallas_call(functools.partial(kernel, cols), out_shape=jax.ShapeDtypeS...]
where the time goes in v5:
time: 40.3 us; the launch traced here: 40.1 us
  Pallas kernels  38.4 us (95%)
  local copies, waits for them, and re-layouts  1.67 us (4%)
    pallas_call x1, Pallas kernels, fused(): pl.pallas_call(functools.partial(kernel, cols), out_shape=jax.ShapeDtypeS...  38.4 us
    unnamed x1, local copies, waits for them, and re-layouts  1.67 us

profile of v5, /device:TPU:0, one launch (start us, length us, event | category | flops | bytes accessed | tf_op | source)
XLA Modules:
  0.0 40.1 jit_solution(16409648960196425079)
XLA Ops:
  0.0 38.4 %shard_map.73 = f32[32,2048]{1,0:T(8,128)} custom-call(bf16[16,4096]{1,0:T(8,128)(2,1)} %draws.1, bf16[2,4,64,1024]{3,2,1,0:T(8,128)(2,1)} %bitcast.2, bf16[2,4,64,1024]{3,2,1,0:T(8,128)(2,1)} %bitcast.3, s32[2,4]{1,0:T(2,128)} %ranks_hbm.1, s32[2,16]{1,0:T(2,128)} %near_hbm.1, f32[2,2048]{1,0:T(2,128)} %row_hbm.1, f32[2,16384]{1,0:T(2,128)} %col_hbm.1), custom_call_target="tpu_custom_call" | custom-call | flops 10000000000 | bytes 10000000 | tf_op jit(solution)/shard_map/pallas_call | solution.py:315
  38.4 1.7 %copy.9 = f32[32,2048]{1,0:T(8,128)} copy(f32[32,2048]{1,0:T(8,128)} %shard_map.73) | data formatting | bytes 524288
